TPU v7x, 32 devices: a whole 2x2x4 slice. The times are simulated.
32 devices in a mesh: dp: 16 (over z, x, core), bfly: 2 (over y).
Axes of the slice: x: 2, y: 2, z: 4, core: 2. Of those that a mesh axis runs over, the one named last changes fastest.
Arguments:
- features: bfloat16 [2048, 8192], P('dp', 'bfly'), may hold values from -6 to 6
- weight: bfloat16 [4, 256, 14336], P(None, 'dp', 'bfly'), may hold values from -0.1875 to 0.1875
- block_table: int32 [4, 56], P(None, 'bfly'), may hold values from 0 to 15
- upstream: bfloat16 [2048, 14336], P('dp', 'bfly'), may hold values from -6 to 6
Outputs:
- activation: bfloat16 [2048, 14336], P('dp', 'bfly')
- input_grad: bfloat16 [2048, 8192], P('dp', 'bfly')
- weight_grad: float32 [4, 256, 14336], P(None, 'dp', 'bfly')
Inputs may be any that keep to these rules, and one draw needn't show every extreme that they name: block_table[s, k] names a feature block within the partner group of hidden block k at section s.
All inputs are finite; a program needn't handle non-finite values.
Results may differ from a plain program's by a relative error of at most 0.0058.
Values may be sent and summed in bfloat16 or wider, within the bound.
A program may use at most 128 MiB of HBM per device.

v0:
```python
import jax
import jax.numpy as jnp
from jax import lax
from jax.sharding import PartitionSpec as P

half_root = 0.7071067811865476
inv_root_tau = 0.3989422804014327


def swapped(block, axis, stride):
    count = lax.axis_size(axis)
    route = []
    for low in range(count):
        high = low | 1 << stride
        if high != low and high < count:
            route += [(low, high), (high, low)]
    return lax.ppermute(block, axis, route)


def gelu_pair(pre_act):
    normal_cdf = 0.5 * (1.0 + lax.erf(pre_act * half_root))
    density = jnp.exp(-0.5 * pre_act * pre_act) * inv_root_tau
    return (pre_act * normal_cdf, normal_cdf + pre_act * density)


def body(features, weight, block_table, upstream):
    tok_rows = features.shape[0]
    sections = weight.shape[0]
    local_width = weight.shape[2]
    hidden_blocks = block_table.shape[1]
    block_size = local_width // hidden_blocks
    groups = lax.axis_size("bfly")
    bit_count = groups.bit_length() - 1
    own_slabs = features.reshape(tok_rows, -1, block_size)
    feat_blocks = own_slabs.shape[1]
    section_bits = [(section_index - 1) % bit_count for section_index in range(1, sections)]
    used_bits = sorted(set(section_bits))
    partner_slabs = {}
    for stride_bit in used_bits:
        partner_slabs[stride_bit] = swapped(own_slabs, "bfly", stride_bit)
    sources = [own_slabs] + [partner_slabs[stride_bit] for stride_bit in section_bits]
    gathered = jnp.stack(
        [
            jnp.take(sources[section_index], block_table[section_index], axis=1)
            for section_index in range(sections)
        ],
        axis=2,
    )
    full_weight = lax.all_gather(weight, "dp", axis=1, tiled=True).reshape(
        sections, -1, hidden_blocks, block_size
    )
    pre_act = jnp.einsum(
        "tjsc,scjd->tjd", gathered, full_weight, preferred_element_type=jnp.float32
    )
    activated, slope_term = gelu_pair(pre_act)
    activation = activated.astype(jnp.bfloat16).reshape(tok_rows, local_width)
    cotangent = upstream.reshape(tok_rows, hidden_blocks, block_size).astype(jnp.float32)
    grad_pre = (cotangent * slope_term).astype(jnp.bfloat16)
    back_terms = jnp.einsum(
        "tjd,scjd->tjsc", grad_pre, full_weight, preferred_element_type=jnp.float32
    )
    columns = jnp.arange(feat_blocks, dtype=jnp.int32)

    def place_blocks(section_index):
        onehot = (block_table[section_index][:, None] == columns[None, :]).astype(jnp.float32)
        return jnp.einsum(
            "jb,tjc->tbc",
            onehot,
            back_terms[:, :, section_index, :],
            precision=lax.Precision.HIGHEST,
        )

    own_share = lax.optimization_barrier(place_blocks(0).astype(jnp.bfloat16)).astype(jnp.float32)
    bit_shares = {}
    for section_index in range(1, sections):
        stride_bit = section_bits[section_index - 1]
        placed = place_blocks(section_index)
        bit_shares[stride_bit] = (
            placed if stride_bit not in bit_shares else bit_shares[stride_bit] + placed
        )
    input_grad = own_share
    for stride_bit in used_bits:
        arrived = swapped(bit_shares[stride_bit].astype(jnp.bfloat16), "bfly", stride_bit)
        input_grad = input_grad + arrived.astype(jnp.float32)
    data_count = lax.axis_size("dp")
    grad_scale = float(tok_rows * data_count) ** (-0.5)
    pieces = []
    for section_index in range(sections):
        grad_term = jnp.einsum(
            "tjc,tjd->cjd",
            gathered[:, :, section_index, :],
            grad_pre,
            preferred_element_type=jnp.float32,
        ).reshape(-1, local_width)
        arrived_rows = lax.all_to_all(grad_term, "dp", split_axis=0, concat_axis=0, tiled=True)
        pieces.append(
            jnp.sum(arrived_rows.reshape(data_count, -1, local_width), axis=0) * grad_scale
        )
    weight_grad = jnp.stack(pieces, axis=0)
    return (activation, input_grad.reshape(tok_rows, -1).astype(jnp.bfloat16), weight_grad)


def solution(mesh):
    return jax.shard_map(
        body,
        mesh=mesh,
        in_specs=(P("dp", "bfly"), P(None, "dp", "bfly"), P(None, "bfly"), P("dp", "bfly")),
        out_specs=(P("dp", "bfly"), P("dp", "bfly"), P(None, "dp", "bfly")),
        check_vma=False,
    )
```

profile of v0, /device:TPU:11, one launch (start us, length us, event | category | flops | bytes accessed | tf_op | source)
XLA Modules:
  0.0 855.9 jit_solution(10047231024623292358)
XLA Ops:
  7.2 0.0 copy-start.7
  7.2 0.0 all-gather.2.cloned.1.call-start
  7.2 2.9 copy.59
  10.1 0.0 all-gather.2.cloned.1.call-update
  10.1 0.0 copy-done.7
  10.1 0.7 copy.56
  10.8 1.3 copy.57
  12.1 1.2 collective-permute-start
  13.4 3.3 copy.63
  16.7 0.0 copy-start.8
  16.7 2.9 copy.64
  19.6 0.0 copy-done.8
  19.6 2.0 gather_fusion
  21.7 1.7 fusion.48
  23.4 13.1 %collective-permute-done = bf16[128,16,256]{2,0,1:T(8,128)(2,1)S(1)} collective-permute-done((bf16[128,16,256]{2,0,1:T(8,128)(2,1)}, bf16[128,16,256]{2,0,1:T(8,128)(2,1)S(1)}, u32[]{:S(2)}, u32[]{:S(2)}) %collective-permute-start) | collective-permute-done | bytes 1048608 | tf_op jit(solution)/shard_map/ppermute | solution.py:17
  36.5 1.9 gather_fusion.3
  38.4 0.0 copy-done
  38.4 2.0 gather_fusion.1
  40.4 1.9 gather_fusion.2
  42.3 1.5 fusion.51
  43.7 0.7 copy-done.3
  44.4 0.6 copy-done.4
  45.0 2.2 fusion.49
  47.2 76.0 %all-gather.2.cloned.1.call-done = bf16[4,256,7168]{2,0,1:T(4,128)(2,1)} async-done(((bf16[4,16,7168]{2,0,1:T(4,128)(2,1)}), bf16[4,256,7168]{2,0,1:T(4,128)(2,1)}) %all-gather.2.cloned.1.call-update) | async-done | bytes 14680080 | tf_op jit(solution)/shard_map/all_gather | solution.py:49
  123.2 23.1 %copy.60 = bf16[4,256,7168]{1,2,0:T(8,128)(2,1)} copy(bf16[4,256,7168]{2,0,1:T(4,128)(2,1)} %all-gather.2.cloned.1.call-done) | data formatting | bytes 29360128 | tf_op jit(solution)/shard_map/all_gather | solution.py:49
  146.3 12.4 %fusion.27 = (bf16[128,28,256]{2,0,1:T(8,128)(2,1)S(1)}, bf16[128,28,256]{2,0,1:T(8,128)(2,1)}) fusion(f32[128,28,256]{2,0,1:T(8,128)} %copy.64, bf16[4,256,28,256]{1,3,2,0:T(8,128)(2,1)} %bitcast.121, bf16[128,28,1,256]{3,0,2,1:T(8,128)(2,1)} %fusion.51, bf16[128,28,1,256]{3,0,2,1:T(8,128)(2,1)} %get-tuple-element.38, ...), kind=kOutput, calls=%fused_computation.30 | convolution fusion | flops 1901068288 | bytes 29360128 | tf_op jit(solution)/shard_map/tjsc,scjd->tjd/dot_general | solution.py:52
  158.7 0.0 copy-done.2
  158.7 4.2 convolution_bitcast_fusion
  162.9 10.3 %copy.77 = f32[256,28,256]{2,1,0:T(8,128)} copy(f32[256,28,256]{0,2,1:T(8,128)} %convolution_bitcast_fusion) | data formatting | bytes 14680064 | tf_op jit(solution)/shard_map/tjc,tjd->cjd/transpose | solution.py:89
  173.2 8.7 %all_to_all.30 = f32[16,16,7168]{2,1,0:T(8,128)} reshape(f32[256,28,256]{2,1,0:T(8,128)} %copy.77) | data formatting | bytes 14680064 | tf_op jit(solution)/shard_map/all_to_all | solution.py:95
  182.0 7.5 all-to-all-start.3
  189.4 5.7 convolution_bitcast_fusion.1
  195.1 10.3 %copy.75 = f32[256,28,256]{2,1,0:T(8,128)} copy(f32[256,28,256]{0,2,1:T(8,128)} %convolution_bitcast_fusion.1) | data formatting | bytes 14680064 | tf_op jit(solution)/shard_map/tjc,tjd->cjd/transpose | solution.py:89
  205.4 8.7 %all_to_all.28 = f32[16,16,7168]{2,1,0:T(8,128)} reshape(f32[256,28,256]{2,1,0:T(8,128)} %copy.75) | data formatting | bytes 14680064 | tf_op jit(solution)/shard_map/all_to_all | solution.py:95
  214.2 135.2 %all-to-all-done.3 = f32[16,16,7168]{2,1,0:T(8,128)} async-done(((f32[16,16,7168]{2,1,0:T(8,128)}), f32[16,16,7168]{2,1,0:T(8,128)}, u32[]{:S(2)}, u32[]{:S(2)}) %all-to-all-start.3) | async-done | bytes 7340064 | tf_op jit(solution)/shard_map/all_to_all | solution.py:95
  349.3 5.4 all-to-all-start.2
  354.7 5.6 convolution_bitcast_fusion.2
  360.3 10.3 %copy.73 = f32[256,28,256]{2,1,0:T(8,128)} copy(f32[256,28,256]{0,2,1:T(8,128)} %convolution_bitcast_fusion.2) | data formatting | bytes 14680064 | tf_op jit(solution)/shard_map/tjc,tjd->cjd/transpose | solution.py:89
  370.6 8.7 %all_to_all.26 = f32[16,16,7168]{2,1,0:T(8,128)} reshape(f32[256,28,256]{2,1,0:T(8,128)} %copy.73) | data formatting | bytes 14680064 | tf_op jit(solution)/shard_map/all_to_all | solution.py:95
  379.3 135.1 %all-to-all-done.2 = f32[16,16,7168]{2,1,0:T(8,128)} async-done(((f32[16,16,7168]{2,1,0:T(8,128)}), f32[16,16,7168]{2,1,0:T(8,128)}, u32[]{:S(2)}, u32[]{:S(2)}) %all-to-all-start.2) | async-done | bytes 7340064 | tf_op jit(solution)/shard_map/all_to_all | solution.py:95
  514.4 4.9 all-to-all-start.1
  519.3 5.6 convolution_bitcast_fusion.3
  524.9 10.3 %copy.71 = f32[256,28,256]{2,1,0:T(8,128)} copy(f32[256,28,256]{0,2,1:T(8,128)} %convolution_bitcast_fusion.3) | data formatting | bytes 14680064 | tf_op jit(solution)/shard_map/tjc,tjd->cjd/transpose | solution.py:89
  535.2 8.7 %all_to_all.24 = f32[16,16,7168]{2,1,0:T(8,128)} reshape(f32[256,28,256]{2,1,0:T(8,128)} %copy.71) | data formatting | bytes 14680064 | tf_op jit(solution)/shard_map/all_to_all | solution.py:95
  544.0 135.2 %all-to-all-done.1 = f32[16,16,7168]{2,1,0:T(8,128)} async-done(((f32[16,16,7168]{2,1,0:T(8,128)}), f32[16,16,7168]{2,1,0:T(8,128)}, u32[]{:S(2)}, u32[]{:S(2)}) %all-to-all-start.1) | async-done | bytes 7340064 | tf_op jit(solution)/shard_map/all_to_all | solution.py:95
  679.2 4.9 all-to-all-start
  684.1 12.4 %fusion.4 = f32[128,28,4,256]{3,0,2,1:T(8,128)} fusion(bf16[4,256,28,256]{1,3,2,0:T(8,128)(2,1)} %bitcast.122, bf16[128,28,256]{2,0,1:T(8,128)(2,1)S(1)} %get-tuple-element.25), kind=kOutput, calls=%fused_computation.8 | convolution fusion | flops 1879048192 | bytes 31195136 | tf_op jit(solution)/shard_map/tjd,scjd->tjsc/dot_general | solution.py:59
  696.6 11.1 %slice_bitcast_fusion.3 = (f32[128,28,256]{2,0,1:T(8,128)}, f32[128,28,256]{2,0,1:T(8,128)}, f32[128,28,256]{2,0,1:T(8,128)}, f32[128,28,256]{2,0,1:T(8,128)}) fusion(f32[128,28,4,256]{3,0,2,1:T(8,128)} %fusion.4), kind=kLoop, calls=%fused_computation.34 | loop fusion | bytes 29360128 | tf_op jit(solution)/shard_map/squeeze | solution.py:69
  707.7 6.2 fusion.14
  713.9 4.1 fusion.16
  718.0 4.6 fusion.45
  722.6 1.3 collective-permute-start.1
  723.9 2.9 copy.62
  726.8 2.9 copy.78
  729.6 6.1 fusion.42
  735.7 11.5 %collective-permute-done.1 = bf16[128,16,256]{2,1,0:T(8,128)(2,1)} collective-permute-done((bf16[128,16,256]{2,1,0:T(8,128)(2,1)S(1)}, bf16[128,16,256]{2,1,0:T(8,128)(2,1)}, u32[]{:S(2)}, u32[]{:S(2)}) %collective-permute-start.1) | collective-permute-done | bytes 1048608 | tf_op jit(solution)/shard_map/ppermute | solution.py:17
  747.2 1.5 add_convert_fusion
  748.7 1.4 copy.89
  750.1 3.5 reduce_sum.39
  753.6 3.5 reduce_sum.38
  757.0 3.5 reduce_sum.37
  760.7 83.3 %all-to-all-done = f32[16,16,7168]{2,1,0:T(8,128)} async-done(((f32[16,16,7168]{2,1,0:T(8,128)}), f32[16,16,7168]{2,1,0:T(8,128)}, u32[]{:S(2)}, u32[]{:S(2)}) %all-to-all-start) | async-done | bytes 7340064 | tf_op jit(solution)/shard_map/all_to_all | solution.py:95
  844.0 3.5 reduce_sum.36
  847.5 1.4 pad_maximum_fusion
  (20 shorter events, 0.2 us)
Async XLA Ops:
  7.2 3.0 copy-start.7
  7.2 116.0 %all-gather.2.cloned.1.call-start = ((), (), s32[]{:S(2)}) async-start(), calls=%async_computation.4 | async-start | bytes 15597568 | tf_op jit(solution)/shard_map/all_gather | solution.py:49
  12.1 24.3 %collective-permute-start = (bf16[128,16,256]{2,0,1:T(8,128)(2,1)}, bf16[128,16,256]{2,0,1:T(8,128)(2,1)S(1)}, u32[]{:S(2)}, u32[]{:S(2)}) collective-permute-start(bf16[128,16,256]{2,0,1:T(8,128)(2,1)} %copy.57), channel_id=1, source_target_pairs={{0,1},{1,0},{2,3},{3,2},{4,5},{5,4},{6,7},{7,6},{8,9},{9,8},{10,11... | collective-permute-start | bytes 3145736 | tf_op jit(solution)/shard_map/ppermute | solution.py:17
  16.7 2.9 copy-start.8
  21.6 16.7 %copy-start = (bf16[28,128,256]{2,1,0:T(8,128)(2,1)}, bf16[28,128,256]{2,1,0:T(8,128)(2,1)S(1)}, u32[]{:S(2)}) copy-start(bf16[28,128,256]{2,1,0:T(8,128)(2,1)S(1)} %gather_fusion) | copy-start | bytes 5505028
  40.4 1.9 copy-start.1
  42.3 2.2 copy-start.3
  42.3 2.7 copy-start.4
  146.3 12.4 %copy-start.2 = (bf16[28,128,256]{2,1,0:T(8,128)(2,1)S(1)}, bf16[28,128,256]{2,1,0:T(8,128)(2,1)}, u32[]{:S(2)}) copy-start(bf16[28,128,256]{2,1,0:T(8,128)(2,1)} %gather_fusion.3) | copy-start | bytes 5505028
  182.0 167.4 %all-to-all-start.3 = ((f32[16,16,7168]{2,1,0:T(8,128)}), f32[16,16,7168]{2,1,0:T(8,128)}, u32[]{:S(2)}, u32[]{:S(2)}) async-start(f32[16,16,7168]{2,1,0:T(8,128)} %all_to_all.30), calls=%async_computation.3 | async-start | bytes 14680064 | tf_op jit(solution)/shard_map/all_to_all | solution.py:95
  349.3 165.1 %all-to-all-start.2 = ((f32[16,16,7168]{2,1,0:T(8,128)}), f32[16,16,7168]{2,1,0:T(8,128)}, u32[]{:S(2)}, u32[]{:S(2)}) async-start(f32[16,16,7168]{2,1,0:T(8,128)} %all_to_all.28), calls=%async_computation.2 | async-start | bytes 14680064 | tf_op jit(solution)/shard_map/all_to_all | solution.py:95
  514.4 164.8 %all-to-all-start.1 = ((f32[16,16,7168]{2,1,0:T(8,128)}), f32[16,16,7168]{2,1,0:T(8,128)}, u32[]{:S(2)}, u32[]{:S(2)}) async-start(f32[16,16,7168]{2,1,0:T(8,128)} %all_to_all.26), calls=%async_computation.1 | async-start | bytes 14680064 | tf_op jit(solution)/shard_map/all_to_all | solution.py:95
  679.2 164.8 %all-to-all-start = ((f32[16,16,7168]{2,1,0:T(8,128)}), f32[16,16,7168]{2,1,0:T(8,128)}, u32[]{:S(2)}, u32[]{:S(2)}) async-start(f32[16,16,7168]{2,1,0:T(8,128)} %all_to_all.24), calls=%async_computation | async-start | bytes 14680064 | tf_op jit(solution)/shard_map/all_to_all | solution.py:95
  707.7 6.2 copy-start.6
  713.9 4.1 copy-start.5
  722.6 24.6 %collective-permute-start.1 = (bf16[128,16,256]{2,1,0:T(8,128)(2,1)S(1)}, bf16[128,16,256]{2,1,0:T(8,128)(2,1)}, u32[]{:S(2)}, u32[]{:S(2)}) collective-permute-start(bf16[128,16,256]{2,1,0:T(8,128)(2,1)S(1)} %fusion.45), channel_id=1, source_target_pairs={{0,1},{1,0},{2,3},{3,2},{4,5},{5,4},{6,7},{7,6},{8,9},{9,8},{10,11... | collective-permute-start | bytes 3145736 | tf_op jit(solution)/shard_map/ppermute | solution.py:17
Sparse Core Ops, SparseCore 0:
  10.3 112.8 all-gather.1
where the time goes:
time: 872 us; the launch traced here: 856 us
  waiting for transfers between devices  589 us (68%)
  local copies, waits for them, and re-layouts  138 us (16%)
  matrix products  66.8 us (8%)
  starting transfers between devices  25.2 us (3%)
  other arithmetic  22.3 us (3%)
  between operations  14.4 us (2%)
    all_to_all x4, waiting for transfers between devices, body(): lax.all_to_all(grad_term, 'dp', split_axis=0, concat_axis=0, tiled=True)  489 us
    all_gather x1, waiting for transfers between devices, body(): lax.all_gather(weight, 'dp', axis=1, tiled=True)  76 us
    transpose x4, local copies, waits for them, and re-layouts, body(): jnp.einsum('tjc,tjd->cjd', gathered[:, :, section_index, :], grad_pre, pr...  41.3 us
    all_to_all x4, local copies, waits for them, and re-layouts, body(): lax.all_to_all(grad_term, 'dp', split_axis=0, concat_axis=0, tiled=True)  34.8 us
    ppermute x2, waiting for transfers between devices, swapped(): return lax.ppermute(block, axis, route)  24.5 us
    all_gather x1, local copies, waits for them, and re-layouts, body(): lax.all_gather(weight, 'dp', axis=1, tiled=True)  23.1 us
    all_to_all x4, starting transfers between devices, body(): lax.all_to_all(grad_term, 'dp', split_axis=0, concat_axis=0, tiled=True)  22.6 us
    dot_general x4, matrix products, body(): jnp.einsum('tjc,tjd->cjd', gathered[:, :, section_index, :], grad_pre, pr...  21.1 us
  transfers between devices with their start and end apart: 7, of which 7 were waited for; matrix products, arithmetic and copies ran while one was open for 16% of the time, Pallas kernels for 0%

commit v1 on v0

v1 whole, which is shorter than its diff:
```python
import functools

import jax
import jax.numpy as jnp
from jax import lax
from jax.experimental import pallas as pl
from jax.experimental.pallas import tpu as pltpu
from jax.sharding import PartitionSpec as P

half_root = 0.7071067811865476
inv_root_tau = 0.3989422804014327
MESH = pl.DeviceIdType.MESH
CHIPS = 8
PARTS = 4
VMEM = pl.BlockSpec(memory_space=pltpu.VMEM)
ANY = pl.BlockSpec(memory_space=pl.ANY)


def swapped(block, axis, stride):
    count = lax.axis_size(axis)
    route = []
    for low in range(count):
        high = low | 1 << stride
        if high != low and high < count:
            route += [(low, high), (high, low)]
    return lax.ppermute(block, axis, route)


def gelu_pair(pre_act):
    normal_cdf = 0.5 * (1.0 + lax.erf(pre_act * half_root))
    density = jnp.exp(-0.5 * pre_act * pre_act) * inv_root_tau
    return (pre_act * normal_cdf, normal_cdf + pre_act * density)


def ring_place():
    dp = lax.axis_index("dp")
    z, x, core = dp // 4, (dp // 2) % 2, dp % 2
    return z + x * (7 - 2 * z), core


def ring_member(place, core):
    place = lax.rem(place + 2 * CHIPS, CHIPS)
    side = place // 4
    return (place + side * (7 - 2 * place)) * 4 + 2 * side + core


def greet(place, core):
    fly = lax.axis_index("bfly")
    barrier = pltpu.get_barrier_semaphore()
    friends = [
        (ring_member(place + 1, core), fly),
        (ring_member(place - 1, core), fly),
        (ring_member(place, 1 - core), fly),
        (ring_member(place, core), 1 - fly),
    ]
    for friend in friends:
        pl.semaphore_signal(barrier, inc=1, device_id=friend, device_id_type=MESH)
    pl.semaphore_wait(barrier, 4)
    return friends


def remote(src, dst, send, recv, where):
    return pltpu.make_async_remote_copy(
        src_ref=src, dst_ref=dst, send_sem=send, recv_sem=recv, device_id=where, device_id_type=MESH
    )


def gather_kernel(w_ref, feat_ref, all_ref, other_ref, own_sem, fly_sem, ring_sem, sib_sem):
    place, core = ring_place()
    up, down, sibling, across = greet(place, core)
    half, width = w_ref.shape[0] // 2, w_ref.shape[1]
    cols = width // PARTS
    fly = remote(feat_ref, other_ref, fly_sem.at[0], fly_sem.at[1], across)
    fly.start()
    own = pltpu.make_async_copy(w_ref, all_ref.at[ring_member(place, core)], own_sem)
    own.start()
    own.wait()

    def view(owner_place, way, part, owner_core):
        return all_ref.at[
            ring_member(owner_place, owner_core), pl.ds(way * half, half), pl.ds(part * cols, cols)
        ]

    def ring(step, way, part):
        piece = view(place - step if way == 0 else place + step, way, part, core)
        return remote(
            piece, piece, ring_sem.at[0, way, part, step], ring_sem.at[1, way, part, step],
            up if way == 0 else down,
        )

    def sib(step, way, part):
        piece = view(place - step if way == 0 else place + step, way, part, core)
        return remote(
            piece, piece, sib_sem.at[0, way, part, step], sib_sem.at[1, way, part, step], sibling
        )

    def at_step(step, carry):
        for part in range(PARTS):
            for way in range(2):
                pl.when(step > 0)(lambda: ring(step - 1, way, part).wait_recv())
                pl.when(step < CHIPS - 1)(lambda: ring(step, way, part).start())
                sib(step, way, part).start()
        return carry

    lax.fori_loop(0, CHIPS, at_step, 0)

    def finish(step, carry):
        for part in range(PARTS):
            for way in range(2):
                pl.when(step < CHIPS - 1)(lambda: ring(step, way, part).wait_send())
                sib(step, way, part).wait()
        return carry

    lax.fori_loop(0, CHIPS, finish, 0)
    fly.wait()


def gather_weights(blob, features):
    rows, width = blob.shape
    return pl.pallas_call(
        gather_kernel,
        name="gather_weights",
        out_shape=(
            jax.ShapeDtypeStruct((2 * CHIPS, rows, width), blob.dtype),
            jax.ShapeDtypeStruct(features.shape, features.dtype),
        ),
        in_specs=[ANY, ANY],
        out_specs=(ANY, ANY),
        scratch_shapes=[
            pltpu.SemaphoreType.DMA,
            pltpu.SemaphoreType.DMA((2,)),
            pltpu.SemaphoreType.DMA((2, 2, PARTS, CHIPS)),
            pltpu.SemaphoreType.DMA((2, 2, PARTS, CHIPS)),
        ],
        compiler_params=pltpu.CompilerParams(collective_id=0, has_side_effects=True),
    )(blob, features)


def scatter_kernel(
    g_ref, shares_ref, out_ref, grad_ref, mine, theirs, arrived, far_share, load_sem, fly_sem, ring_sem, sib_sem
):
    place, core = ring_place()
    up, down, sibling, across = greet(place, core)
    half, width = mine.shape[2], mine.shape[3]
    cols = width // PARTS
    fly = remote(shares_ref.at[1], far_share, fly_sem.at[0], fly_sem.at[1], across)

    def target(step, way):
        return place - 1 - step if way == 0 else place + 1 + step

    def span(part):
        return pl.ds(part * cols, cols)

    def load(step, way, part):
        return pltpu.make_async_copy(
            g_ref.at[ring_member(target(step, way), core), pl.ds(way * half, half), span(part)],
            mine.at[way, step, :, span(part)],
            load_sem.at[way, part, step],
        )

    def sib(step, way, part):
        return remote(
            g_ref.at[ring_member(target(step, way), 1 - core), pl.ds(way * half, half), span(part)],
            theirs.at[way, step, :, span(part)],
            sib_sem.at[0, way, part, step],
            sib_sem.at[1, way, part, step],
            sibling,
        )

    def ring(step, way, part):
        return remote(
            mine.at[way, step, :, span(part)],
            arrived.at[way, step, :, span(part)],
            ring_sem.at[0, way, part, step],
            ring_sem.at[1, way, part, step],
            up if way == 0 else down,
        )

    def begin(step, carry):
        for part in range(PARTS):
            for way in range(2):
                sib(step, way, part).start()
                load(step, way, part).start()
        return carry

    lax.fori_loop(0, CHIPS, begin, 0)
    fly.start()

    def wide(ref, way, step, row, part):
        return ref[way, step, pl.ds(row * 16, 16), span(part)].astype(jnp.float32)

    def at_step(step, carry):
        for part in range(PARTS):
            for way in range(2):
                load(step, way, part).wait()
                sib(step, way, part).wait_recv()

                @pl.when(step == 0)
                def _():
                    for row in range(half // 16):
                        total = wide(mine, way, step, row, part) + wide(theirs, way, step, row, part)
                        mine[way, step, pl.ds(row * 16, 16), span(part)] = total.astype(mine.dtype)

                @pl.when(step > 0)
                def _():
                    ring(step - 1, way, part).wait_recv()

                @pl.when(jnp.logical_and(step > 0, step < CHIPS - 1))
                def _():
                    for row in range(half // 16):
                        total = wide(mine, way, step, row, part) + wide(theirs, way, step, row, part)
                        total = total + wide(arrived, way, step - 1, row, part)
                        mine[way, step, pl.ds(row * 16, 16), span(part)] = total.astype(mine.dtype)

                @pl.when(step < CHIPS - 1)
                def _():
                    ring(step, way, part).start()

        return carry

    lax.fori_loop(0, CHIPS, at_step, 0)
    last = CHIPS - 1
    for part in range(PARTS):
        for way in range(2):
            for row in range(half // 16):
                total = wide(mine, way, last, row, part) + wide(theirs, way, last, row, part)
                total = total + wide(arrived, way, last - 1, row, part)
                out_ref[pl.ds(way * half + row * 16, 16), span(part)] = total
    fly.wait()
    grad_ref[...] = (
        shares_ref[0].astype(jnp.float32) + far_share[...].astype(jnp.float32)
    ).astype(grad_ref.dtype)

    def finish(step, carry):
        for part in range(PARTS):
            for way in range(2):
                pl.when(step < CHIPS - 1)(lambda: ring(step, way, part).wait_send())
                sib(step, way, part).wait_send()
        return carry

    lax.fori_loop(0, CHIPS, finish, 0)


def scatter_grads(grads, shares):
    count, rows, width = grads.shape
    half = rows // 2
    return pl.pallas_call(
        scatter_kernel,
        name="scatter_grads",
        out_shape=(
            jax.ShapeDtypeStruct((rows, width), jnp.float32),
            jax.ShapeDtypeStruct(shares.shape[1:], shares.dtype),
        ),
        in_specs=[ANY, VMEM],
        out_specs=(VMEM, VMEM),
        scratch_shapes=[
            pltpu.VMEM((2, CHIPS, half, width), grads.dtype),
            pltpu.VMEM((2, CHIPS, half, width), grads.dtype),
            pltpu.VMEM((2, CHIPS - 1, half, width), grads.dtype),
            pltpu.VMEM(shares.shape[1:], shares.dtype),
            pltpu.SemaphoreType.DMA((2, PARTS, CHIPS)),
            pltpu.SemaphoreType.DMA((2,)),
            pltpu.SemaphoreType.DMA((2, 2, PARTS, CHIPS)),
            pltpu.SemaphoreType.DMA((2, 2, PARTS, CHIPS)),
        ],
        compiler_params=pltpu.CompilerParams(
            collective_id=1, has_side_effects=True, vmem_limit_bytes=48 * 2**20
        ),
    )(grads, shares)


def block_kernel(source_of, scale, table_ref, *refs):
    sources = max(source_of) + 1
    feats = refs[:sources]
    w_ref, up_ref, act_ref, g_ref, share_ref, total = refs[sources:]
    sections = len(source_of)
    count, rows = w_ref.shape[0], w_ref.shape[1] // sections
    block = w_ref.shape[2]
    k = pl.program_id(0)

    @pl.when(k == 0)
    def _():
        total[...] = jnp.zeros_like(total)

    spans = [pl.ds(pl.multiple_of(table_ref[s, k] * block, block), block) for s in range(sections)]
    taken = [feats[source_of[s]][:, spans[s]] for s in range(sections)]
    weights = [w_ref[:, s * rows : (s + 1) * rows, :].reshape(-1, block) for s in range(sections)]
    pre_act = jnp.dot(taken[0], weights[0], preferred_element_type=jnp.float32)
    for s in range(1, sections):
        pre_act = pre_act + jnp.dot(taken[s], weights[s], preferred_element_type=jnp.float32)
    activated, slope = gelu_pair(pre_act)
    act_ref[...] = activated.astype(act_ref.dtype)
    grad_pre = (up_ref[...].astype(jnp.float32) * slope).astype(jnp.bfloat16)
    for s in range(sections):
        back = lax.dot_general(
            grad_pre, weights[s], (((1,), (1,)), ((), ())), preferred_element_type=jnp.float32
        )
        total[source_of[s], :, spans[s]] += back
        grad = lax.dot_general(
            taken[s], grad_pre, (((0,), (0,)), ((), ())), preferred_element_type=jnp.float32
        )
        g_ref[:, s * rows : (s + 1) * rows, :] = (grad * scale).astype(g_ref.dtype).reshape(
            count, rows, block
        )

    @pl.when(k == pl.num_programs(0) - 1)
    def _():
        share_ref[...] = total[...].astype(share_ref.dtype)


def block_math(source_of, scale, table, feats, w_all, upstream):
    tok_rows, width = upstream.shape
    count, rows, _ = w_all.shape
    hidden = table.shape[1]
    block = width // hidden
    wide = feats[0].shape[1]
    sources = len(feats)
    flops = 2 * 3 * tok_rows * width * count * rows
    return pl.pallas_call(
        functools.partial(block_kernel, source_of, scale),
        name="block_math",
        grid_spec=pltpu.PrefetchScalarGridSpec(
            num_scalar_prefetch=1,
            grid=(hidden,),
            in_specs=[pl.BlockSpec((tok_rows, wide), lambda k, t: (0, 0))] * sources
            + [
                pl.BlockSpec((count, rows, block), lambda k, t: (0, 0, k)),
                pl.BlockSpec((tok_rows, block), lambda k, t: (0, k)),
            ],
            out_specs=[
                pl.BlockSpec((tok_rows, block), lambda k, t: (0, k)),
                pl.BlockSpec((count, rows, block), lambda k, t: (0, 0, k)),
                pl.BlockSpec((sources, tok_rows, wide), lambda k, t: (0, 0, 0)),
            ],
            scratch_shapes=[pltpu.VMEM((sources, tok_rows, wide), jnp.float32)],
        ),
        out_shape=(
            jax.ShapeDtypeStruct((tok_rows, width), jnp.bfloat16),
            jax.ShapeDtypeStruct((count, rows, width), jnp.bfloat16),
            jax.ShapeDtypeStruct((sources, tok_rows, wide), jnp.bfloat16),
        ),
        compiler_params=pltpu.CompilerParams(
            dimension_semantics=("arbitrary",), vmem_limit_bytes=40 * 2**20
        ),
        cost_estimate=pl.CostEstimate(
            flops=flops, bytes_accessed=4 * count * rows * width, transcendentals=2 * tok_rows * width
        ),
    )(table, *feats, w_all, upstream)


def body(on_ring, features, weight, block_table, upstream):
    tok_rows = features.shape[0]
    sections, rows, local_width = weight.shape
    groups = lax.axis_size("bfly")
    bit_count = groups.bit_length() - 1
    data_count = lax.axis_size("dp")
    scale = float(tok_rows * data_count) ** (-0.5)
    section_bits = [(section_index - 1) % bit_count for section_index in range(1, sections)]
    used_bits = sorted(set(section_bits))
    source_of = (0,) + tuple(1 + used_bits.index(bit) for bit in section_bits)
    if on_ring:
        blob = weight.reshape(sections * rows, local_width)
        w_all, partner = gather_weights(blob, features)
        activation, grads, shares = block_math(
            source_of, scale, block_table, [features, partner], w_all, upstream
        )
        weight_grad, input_grad = scatter_grads(grads, shares)
        return (activation, input_grad, weight_grad.reshape(weight.shape))
    feats = [features] + [swapped(features, "bfly", bit) for bit in used_bits]
    w_all = lax.all_gather(weight, "dp", axis=1, tiled=True).reshape(1, -1, local_width)
    activation, grads, shares = block_math(source_of, scale, block_table, feats, w_all, upstream)
    input_grad = shares[0].astype(jnp.float32)
    for at, bit in enumerate(used_bits):
        input_grad = input_grad + swapped(shares[1 + at], "bfly", bit).astype(jnp.float32)
    weight_grad = lax.psum_scatter(
        grads.reshape(sections, -1, local_width).astype(jnp.float32), "dp", scatter_dimension=1, tiled=True
    )
    return (activation, input_grad.astype(jnp.bfloat16), weight_grad)


def solution(mesh):
    on_ring = mesh.shape["dp"] == 2 * CHIPS and mesh.shape["bfly"] == 2
    return jax.shard_map(
        functools.partial(body, on_ring),
        mesh=mesh,
        in_specs=(P("dp", "bfly"), P(None, "dp", "bfly"), P(None, "bfly"), P("dp", "bfly")),
        out_specs=(P("dp", "bfly"), P("dp", "bfly"), P(None, "dp", "bfly")),
        check_vma=False,
    )
```

time: 872 us -> 222 us (0.25); the launches traced: 856 us -> 219 us
  waiting for transfers between devices: 589 us -> 0 us
  Pallas kernels: 0 us -> 213 us
  local copies, waits for them, and re-layouts: 138 us -> 4.93 us
  matrix products: 66.8 us -> 0 us
  starting transfers between devices: 25.2 us -> 0 us
  other arithmetic: 22.3 us -> 0 us
  between operations: 14.4 us -> 0.69 us
    all_to_all x4 -> x0, waiting for transfers between devices: 489 us -> none  [body(): lax.all_to_all(grad_term, 'dp', split_axis=0, concat_axis=0, tiled=True)]
    pallas_call x0 -> x3, Pallas kernels: none -> 213 us  [the longest x1 106 us: gather_weights(): pl.pallas_call(gather_kernel, name='gather_weights', out_shape=(jax.Shape...]
    all_gather x1 -> x0, waiting for transfers between devices: 76 us -> none  [body(): lax.all_gather(weight, 'dp', axis=1, tiled=True)]
    dot_general x10 -> x0, matrix products: 66.8 us -> none  [the longest x4 21.1 us: body(): jnp.einsum('tjc,tjd->cjd', gathered[:, :, section_index, :], grad_pre, pr...]
    transpose x4 -> x0, local copies, waits for them, and re-layouts: 41.3 us -> none  [body(): jnp.einsum('tjc,tjd->cjd', gathered[:, :, section_index, :], grad_pre, pr...]
    all_to_all x4 -> x0, local copies, waits for them, and re-layouts: 34.8 us -> none  [body(): lax.all_to_all(grad_term, 'dp', split_axis=0, concat_axis=0, tiled=True)]
    ppermute x2 -> x0, waiting for transfers between devices: 24.5 us -> none  [swapped(): return lax.ppermute(block, axis, route)]
    all_gather x1 -> x0, local copies, waits for them, and re-layouts: 23.1 us -> none  [body(): lax.all_gather(weight, 'dp', axis=1, tiled=True)]
  transfers between devices with their start and end apart: 7 -> 0, of which waited for: 7 -> 0; matrix products, arithmetic and copies ran while one was open for 16% -> 0% of each run, Pallas kernels for 0% -> 0%
where the time goes in v1:
time: 222 us; the launch traced here: 219 us
  Pallas kernels  213 us (96%)
  local copies, waits for them, and re-layouts  4.93 us (2%)
    pallas_call x1, Pallas kernels, gather_weights(): pl.pallas_call(gather_kernel, name='gather_weights', out_shape=(jax.Shape...  106 us
    pallas_call x1, Pallas kernels, scatter_grads(): pl.pallas_call(scatter_kernel, name='scatter_grads', out_shape=(jax.Shape...  76.9 us
    pallas_call x1, Pallas kernels, block_math(): pl.pallas_call(functools.partial(block_kernel, source_of, scale), name='b...  30.2 us
    unnamed x10, local copies, waits for them, and re-layouts  4.93 us

profile of v1, /device:TPU:11, one launch (start us, length us, event | category | flops | bytes accessed | tf_op | source)
XLA Modules:
  0.0 218.6 jit_solution(743483077595195185)
XLA Ops:
  0.6 0.0 copy-start
  0.6 0.0 copy-start.3
  0.7 106.0 %gather_weights.1 = (bf16[16,64,7168]{2,1,0:T(8,128)(2,1)}, bf16[128,4096]{1,0:T(8,128)(2,1)}) custom-call(bf16[64,7168]{1,0:T(8,128)(2,1)} %bitcast.3, bf16[128,4096]{1,0:T(8,128)(2,1)} %refs_0_.1), custom_call_target="tpu_custom_call" | custom-call | tf_op jit(solution)/shard_map/gather_weights/pallas_call | solution.py:120
  106.6 0.0 copy-done
  106.6 0.0 copy-done.3
  106.6 0.0 copy-start.1
  106.7 1.5 copy-done.1
  108.1 0.0 copy-start.2
  108.1 1.2 copy-done.2
  109.4 30.2 %block_math.1 = (bf16[128,7168]{1,0:T(8,128)(2,1)}, bf16[16,64,7168]{2,1,0:T(8,128)(2,1)}, bf16[2,128,4096]{2,1,0:T(8,128)(2,1)S(1)}) custom-call(s32[4,28]{1,0:T(4,128)S(1)} %copy-done.3, bf16[128,4096]{1,0:T(8,128)(2,1)S(1)} %copy-done, bf16[128,4096]{1,0:T(8,128)(2,1)S(1)} %copy-done.2, bf16[16,64,7168]{2,1,0:T(8,128)(2,1)} %get-tuple-element.11.refs_2_, ...), custom_call_target="tpu_custom_call" | custom-call | flops 5637144576 | bytes 29360128 | tf_op jit(solution)/shard_map/block_math/pallas_call | solution.py:319
  139.5 76.9 %scatter_grads.1 = (f32[64,7168]{1,0:T(8,128)S(1)}, bf16[128,4096]{1,0:T(8,128)(2,1)S(1)}) custom-call(bf16[16,64,7168]{2,1,0:T(8,128)(2,1)} %get-tuple-element.13.g_ref, bf16[2,128,4096]{2,1,0:T(8,128)(2,1)S(1)} %get-tuple-element.14.shares_ref), custom_call_target="tpu_custom_call" | custom-call | tf_op jit(solution)/shard_map/scatter_grads/pallas_call | solution.py:247
  216.4 1.0 copy.9
  217.4 1.2 copy.10
Async XLA Ops:
  0.6 106.0 %copy-start = (bf16[128,4096]{1,0:T(8,128)(2,1)S(1)}, bf16[128,4096]{1,0:T(8,128)(2,1)}, u32[]{:S(2)}) copy-start(bf16[128,4096]{1,0:T(8,128)(2,1)} %refs_0_.1) | copy-start | bytes 3145732
  0.6 106.0 %copy-start.3 = (s32[4,28]{1,0:T(4,128)S(1)}, s32[4,28]{1,0:T(4,128)}, u32[]{:S(2)}) copy-start(s32[4,28]{1,0:T(4,128)} %table_ref.1) | copy-start | bytes 1348
  106.6 1.5 copy-start.1
  108.1 1.2 copy-start.2

commit v2 on v1

--- a/solution.py
+++ b/solution.py
@@ -11,7 +11,8 @@
 inv_root_tau = 0.3989422804014327
 MESH = pl.DeviceIdType.MESH
 CHIPS = 8
-PARTS = 4
+LOTS = 4
+PARTS = 2
 VMEM = pl.BlockSpec(memory_space=pltpu.VMEM)
 ANY = pl.BlockSpec(memory_space=pl.ANY)
 
@@ -125,14 +126,14 @@
             jax.ShapeDtypeStruct(features.shape, features.dtype),
         ),
         in_specs=[ANY, ANY],
-        out_specs=(ANY, ANY),
+        out_specs=(VMEM, ANY),
         scratch_shapes=[
             pltpu.SemaphoreType.DMA,
             pltpu.SemaphoreType.DMA((2,)),
             pltpu.SemaphoreType.DMA((2, 2, PARTS, CHIPS)),
             pltpu.SemaphoreType.DMA((2, 2, PARTS, CHIPS)),
         ],
-        compiler_params=pltpu.CompilerParams(collective_id=0, has_side_effects=True),
+        compiler_params=pltpu.CompilerParams(collective_id=0, has_side_effects=True, vmem_limit_bytes=40 * 2**20),
     )(blob, features)
 
 
@@ -272,38 +273,52 @@
 def block_kernel(source_of, scale, table_ref, *refs):
     sources = max(source_of) + 1
     feats = refs[:sources]
-    w_ref, up_ref, act_ref, g_ref, share_ref, total = refs[sources:]
+    w_ref, up_ref, act_ref, g_ref, share_ref, total, flipped = refs[sources:]
     sections = len(source_of)
     count, rows = w_ref.shape[0], w_ref.shape[1] // sections
-    block = w_ref.shape[2]
-    k = pl.program_id(0)
-
-    @pl.when(k == 0)
+    tokens, wide = feats[0].shape
+    lots = table_ref.shape[1] // pl.num_programs(0)
+    block = w_ref.shape[2] // lots
+    at = pl.program_id(0)
+
+    @pl.when(at == 0)
     def _():
         total[...] = jnp.zeros_like(total)
-
-    spans = [pl.ds(pl.multiple_of(table_ref[s, k] * block, block), block) for s in range(sections)]
-    taken = [feats[source_of[s]][:, spans[s]] for s in range(sections)]
-    weights = [w_ref[:, s * rows : (s + 1) * rows, :].reshape(-1, block) for s in range(sections)]
-    pre_act = jnp.dot(taken[0], weights[0], preferred_element_type=jnp.float32)
-    for s in range(1, sections):
-        pre_act = pre_act + jnp.dot(taken[s], weights[s], preferred_element_type=jnp.float32)
-    activated, slope = gelu_pair(pre_act)
-    act_ref[...] = activated.astype(act_ref.dtype)
-    grad_pre = (up_ref[...].astype(jnp.float32) * slope).astype(jnp.bfloat16)
-    for s in range(sections):
-        back = lax.dot_general(
-            grad_pre, weights[s], (((1,), (1,)), ((), ())), preferred_element_type=jnp.float32
-        )
-        total[source_of[s], :, spans[s]] += back
-        grad = lax.dot_general(
-            taken[s], grad_pre, (((0,), (0,)), ((), ())), preferred_element_type=jnp.float32
-        )
-        g_ref[:, s * rows : (s + 1) * rows, :] = (grad * scale).astype(g_ref.dtype).reshape(
-            count, rows, block
-        )
-
-    @pl.when(k == pl.num_programs(0) - 1)
+        for source in range(sources):
+            for b in range(wide // block):
+                span = slice(b * block, (b + 1) * block)
+                flipped[source, span, :] = feats[source][:, span].T
+
+    for lot in range(lots):
+        k = at * lots + lot
+        col = slice(lot * block, (lot + 1) * block)
+        spans = [
+            pl.ds(pl.multiple_of(table_ref[s, k] * block, block), block) for s in range(sections)
+        ]
+        weights = [
+            w_ref[:, s * rows : (s + 1) * rows, col].reshape(-1, block) for s in range(sections)
+        ]
+        pre_act = jnp.zeros((tokens, block), jnp.float32)
+        for s in range(sections):
+            pre_act = pre_act + jnp.dot(
+                feats[source_of[s]][:, spans[s]], weights[s], preferred_element_type=jnp.float32
+            )
+        activated, slope = gelu_pair(pre_act)
+        act_ref[:, col] = activated.astype(act_ref.dtype)
+        grad_pre = (up_ref[:, col].astype(jnp.float32) * slope).astype(jnp.bfloat16)
+        for s in range(sections):
+            back = lax.dot_general(
+                grad_pre, weights[s], (((1,), (1,)), ((), ())), preferred_element_type=jnp.float32
+            )
+            total[source_of[s], :, spans[s]] += back
+            grad = jnp.dot(
+                flipped[source_of[s], spans[s], :], grad_pre, preferred_element_type=jnp.float32
+            )
+            g_ref[:, s * rows : (s + 1) * rows, col] = (
+                (grad * scale).astype(g_ref.dtype).reshape(count, rows, block)
+            )
+
+    @pl.when(at == pl.num_programs(0) - 1)
     def _():
         share_ref[...] = total[...].astype(share_ref.dtype)
 
@@ -312,7 +327,8 @@
     tok_rows, width = upstream.shape
     count, rows, _ = w_all.shape
     hidden = table.shape[1]
-    block = width // hidden
+    lots = LOTS if hidden % LOTS == 0 else 1
+    span = width // hidden * lots
     wide = feats[0].shape[1]
     sources = len(feats)
     flops = 2 * 3 * tok_rows * width * count * rows
@@ -321,18 +337,21 @@
         name="block_math",
         grid_spec=pltpu.PrefetchScalarGridSpec(
             num_scalar_prefetch=1,
-            grid=(hidden,),
+            grid=(hidden // lots,),
             in_specs=[pl.BlockSpec((tok_rows, wide), lambda k, t: (0, 0))] * sources
             + [
-                pl.BlockSpec((count, rows, block), lambda k, t: (0, 0, k)),
-                pl.BlockSpec((tok_rows, block), lambda k, t: (0, k)),
+                pl.BlockSpec((count, rows, span), lambda k, t: (0, 0, k)),
+                pl.BlockSpec((tok_rows, span), lambda k, t: (0, k)),
             ],
             out_specs=[
-                pl.BlockSpec((tok_rows, block), lambda k, t: (0, k)),
-                pl.BlockSpec((count, rows, block), lambda k, t: (0, 0, k)),
+                pl.BlockSpec((tok_rows, span), lambda k, t: (0, k)),
+                pl.BlockSpec((count, rows, span), lambda k, t: (0, 0, k)),
                 pl.BlockSpec((sources, tok_rows, wide), lambda k, t: (0, 0, 0)),
             ],
-            scratch_shapes=[pltpu.VMEM((sources, tok_rows, wide), jnp.float32)],
+            scratch_shapes=[
+                pltpu.VMEM((sources, tok_rows, wide), jnp.float32),
+                pltpu.VMEM((sources, wide, tok_rows), jnp.bfloat16),
+            ],
         ),
         out_shape=(
             jax.ShapeDtypeStruct((tok_rows, width), jnp.bfloat16),

time: 222 us -> 187 us (0.84)
  Pallas kernels: 213 us -> 178 us
    pallas_call x1, Pallas kernels: 106 us -> 81 us  [gather_weights(): pl.pallas_call(gather_kernel, name='gather_weights', out_shape=(jax.Shape...]
    pallas_call x1, Pallas kernels: 30.2 us -> 21.5 us  [block_math(): pl.pallas_call(functools.partial(block_kernel, source_of, scale), name='b...]
    unnamed x10 -> x12, local copies, waits for them, and re-layouts: 4.93 us -> 6.1 us
where the time goes in v2:
time: 187 us; the launch traced here: 185 us
  Pallas kernels  178 us (95%)
  local copies, waits for them, and re-layouts  6.1 us (3%)
    pallas_call x1, Pallas kernels, gather_weights(): pl.pallas_call(gather_kernel, name='gather_weights', out_shape=(jax.Shape...  81 us
    pallas_call x1, Pallas kernels, scatter_grads(): pl.pallas_call(scatter_kernel, name='scatter_grads', out_shape=(jax.Shape...  75.5 us
    pallas_call x1, Pallas kernels, block_math(): pl.pallas_call(functools.partial(block_kernel, source_of, scale), name='b...  21.5 us
    unnamed x12, local copies, waits for them, and re-layouts  6.1 us

profile of v2, /device:TPU:11, one launch (start us, length us, event | category | flops | bytes accessed | tf_op | source)
XLA Modules:
  0.0 184.8 jit_solution(4510951557098233705)
XLA Ops:
  0.6 0.0 copy-start
  0.6 1.2 copy-done
  1.9 0.0 copy-start.2
  1.9 1.2 copy-done.2
  3.0 0.0 copy-start.1
  3.0 0.0 copy-start.4
  3.0 81.0 %gather_weights.1 = (bf16[16,64,7168]{2,1,0:T(8,128)(2,1)}, bf16[128,4096]{1,0:T(8,128)(2,1)S(1)}) custom-call(bf16[64,7168]{1,0:T(8,128)(2,1)S(1)} %bitcast.3, bf16[128,4096]{1,0:T(8,128)(2,1)S(1)} %copy-done), custom_call_target="tpu_custom_call" | custom-call | tf_op jit(solution)/shard_map/gather_weights/pallas_call | solution.py:121
  84.0 0.0 copy-done.1
  84.0 0.0 copy-done.4
  84.0 0.0 copy-start.3
  84.0 1.5 copy-done.3
  85.5 21.5 %block_math.1 = (bf16[128,7168]{1,0:T(8,128)(2,1)}, bf16[16,64,7168]{2,1,0:T(8,128)(2,1)}, bf16[2,128,4096]{2,1,0:T(8,128)(2,1)S(1)}) custom-call(s32[4,28]{1,0:T(4,128)S(1)} %copy-done.4, bf16[128,4096]{1,0:T(8,128)(2,1)S(1)} %copy-done.1, bf16[128,4096]{1,0:T(8,128)(2,1)S(1)} %get-tuple-element.10.refs_1_, ...), custom_call_target="tpu_custom_call" | custom-call | flops 5637144576 | bytes 29360128 | tf_op jit(solution)/shard_map/block_math/pallas_call | solution.py:335
  107.0 75.5 %scatter_grads.1 = (f32[64,7168]{1,0:T(8,128)S(1)}, bf16[128,4096]{1,0:T(8,128)(2,1)S(1)}) custom-call(bf16[16,64,7168]{2,1,0:T(8,128)(2,1)} %get-tuple-element.13.g_ref, bf16[2,128,4096]{2,1,0:T(8,128)(2,1)S(1)} %get-tuple-element.14.shares_ref), custom_call_target="tpu_custom_call" | custom-call | tf_op jit(solution)/shard_map/scatter_grads/pallas_call | solution.py:248
  182.6 1.0 copy.9
  183.5 1.2 copy.10
Async XLA Ops:
  0.6 1.2 copy-start
  1.9 1.2 copy-start.2
  3.0 81.0 %copy-start.1 = (bf16[128,4096]{1,0:T(8,128)(2,1)S(1)}, bf16[128,4096]{1,0:T(8,128)(2,1)}, u32[]{:S(2)}) copy-start(bf16[128,4096]{1,0:T(8,128)(2,1)} %refs_0_.1) | copy-start | bytes 3145732
  3.0 81.0 %copy-start.4 = (s32[4,28]{1,0:T(4,128)S(1)}, s32[4,28]{1,0:T(4,128)}, u32[]{:S(2)}) copy-start(s32[4,28]{1,0:T(4,128)} %table_ref.1) | copy-start | bytes 1348
  84.0 1.5 copy-start.3

commit v3 on v2

--- a/solution.py
+++ b/solution.py
@@ -66,19 +66,19 @@
     )
 
 
-def gather_kernel(w_ref, feat_ref, all_ref, other_ref, own_sem, fly_sem, ring_sem, sib_sem):
+def gather_kernel(w_ref, feat_ref, all_ref, other_ref, held, own_sem, fly_sem, ring_sem, sib_sem, out_sem):
     place, core = ring_place()
     up, down, sibling, across = greet(place, core)
     half, width = w_ref.shape[0] // 2, w_ref.shape[1]
     cols = width // PARTS
     fly = remote(feat_ref, other_ref, fly_sem.at[0], fly_sem.at[1], across)
     fly.start()
-    own = pltpu.make_async_copy(w_ref, all_ref.at[ring_member(place, core)], own_sem)
+    own = pltpu.make_async_copy(w_ref, held.at[ring_member(place, core)], own_sem)
     own.start()
     own.wait()
 
-    def view(owner_place, way, part, owner_core):
-        return all_ref.at[
+    def view(owner_place, way, part, owner_core, ref=held):
+        return ref.at[
             ring_member(owner_place, owner_core), pl.ds(way * half, half), pl.ds(part * cols, cols)
         ]
 
@@ -95,21 +95,42 @@
             piece, piece, sib_sem.at[0, way, part, step], sib_sem.at[1, way, part, step], sibling
         )
 
+    def out(step, way, part, other):
+        owner = place - step if way == 0 else place + step
+        owner_core = 1 - core if other else core
+        return pltpu.make_async_copy(
+            view(owner, way, part, owner_core),
+            view(owner, way, part, owner_core, all_ref),
+            out_sem.at[other, way, part, step],
+        )
+
+    def from_sibling(step, way, part):
+        sib(step, way, part).wait_recv()
+        out(step, way, part, 1).start()
+
     def at_step(step, carry):
         for part in range(PARTS):
             for way in range(2):
                 pl.when(step > 0)(lambda: ring(step - 1, way, part).wait_recv())
                 pl.when(step < CHIPS - 1)(lambda: ring(step, way, part).start())
                 sib(step, way, part).start()
+                out(step, way, part, 0).start()
+                pl.when(step >= 2)(lambda: from_sibling(step - 2, way, part))
         return carry
 
     lax.fori_loop(0, CHIPS, at_step, 0)
+    for step in (CHIPS - 2, CHIPS - 1):
+        for part in range(PARTS):
+            for way in range(2):
+                from_sibling(step, way, part)
 
     def finish(step, carry):
         for part in range(PARTS):
             for way in range(2):
                 pl.when(step < CHIPS - 1)(lambda: ring(step, way, part).wait_send())
-                sib(step, way, part).wait()
+                sib(step, way, part).wait_send()
+                out(step, way, part, 0).wait()
+                out(step, way, part, 1).wait()
         return carry
 
     lax.fori_loop(0, CHIPS, finish, 0)
@@ -126,10 +147,12 @@
             jax.ShapeDtypeStruct(features.shape, features.dtype),
         ),
         in_specs=[ANY, ANY],
-        out_specs=(VMEM, ANY),
+        out_specs=(ANY, ANY),
         scratch_shapes=[
+            pltpu.VMEM((2 * CHIPS, rows, width), blob.dtype),
             pltpu.SemaphoreType.DMA,
             pltpu.SemaphoreType.DMA((2,)),
+            pltpu.SemaphoreType.DMA((2, 2, PARTS, CHIPS)),
             pltpu.SemaphoreType.DMA((2, 2, PARTS, CHIPS)),
             pltpu.SemaphoreType.DMA((2, 2, PARTS, CHIPS)),
         ],

time: 187 us -> 183 us (0.979)
  Pallas kernels: 178 us -> 173 us
    pallas_call x1, Pallas kernels: 81 us -> 77 us  [gather_weights(): pl.pallas_call(gather_kernel, name='gather_weights', out_shape=(jax.Shape...]
where the time goes in v3:
time: 183 us; the launch traced here: 180 us
  Pallas kernels  173 us (95%)
  local copies, waits for them, and re-layouts  6.1 us (3%)
    pallas_call x1, Pallas kernels, gather_weights(): pl.pallas_call(gather_kernel, name='gather_weights', out_shape=(jax.Shape...  77 us
    pallas_call x1, Pallas kernels, scatter_grads(): pl.pallas_call(scatter_kernel, name='scatter_grads', out_shape=(jax.Shape...  74.4 us
    pallas_call x1, Pallas kernels, block_math(): pl.pallas_call(functools.partial(block_kernel, source_of, scale), name='b...  21.5 us
    unnamed x12, local copies, waits for them, and re-layouts  6.1 us

profile of v3, /device:TPU:11, one launch (start us, length us, event | category | flops | bytes accessed | tf_op | source)
XLA Modules:
  0.0 179.7 jit_solution(11995131084539542035)
XLA Ops:
  0.6 0.0 copy-start
  0.6 1.2 copy-done
  1.9 0.0 copy-start.2
  1.9 1.2 copy-done.2
  3.0 0.0 copy-start.1
  3.0 0.0 copy-start.4
  3.0 77.0 %gather_weights.1 = (bf16[16,64,7168]{2,1,0:T(8,128)(2,1)}, bf16[128,4096]{1,0:T(8,128)(2,1)S(1)}) custom-call(bf16[64,7168]{1,0:T(8,128)(2,1)S(1)} %bitcast.3, bf16[128,4096]{1,0:T(8,128)(2,1)S(1)} %copy-done), custom_call_target="tpu_custom_call" | custom-call | tf_op jit(solution)/shard_map/gather_weights/pallas_call | solution.py:142
  80.1 0.0 copy-done.1
  80.1 0.0 copy-done.4
  80.1 0.0 copy-start.3
  80.1 1.5 copy-done.3
  81.6 21.5 %block_math.1 = (bf16[128,7168]{1,0:T(8,128)(2,1)}, bf16[16,64,7168]{2,1,0:T(8,128)(2,1)}, bf16[2,128,4096]{2,1,0:T(8,128)(2,1)S(1)}) custom-call(s32[4,28]{1,0:T(4,128)S(1)} %copy-done.4, bf16[128,4096]{1,0:T(8,128)(2,1)S(1)} %copy-done.1, bf16[128,4096]{1,0:T(8,128)(2,1)S(1)} %get-tuple-element.10.refs_1_, ...), custom_call_target="tpu_custom_call" | custom-call | flops 5637144576 | bytes 29360128 | tf_op jit(solution)/shard_map/block_math/pallas_call | solution.py:358
  103.1 74.4 %scatter_grads.1 = (f32[64,7168]{1,0:T(8,128)S(1)}, bf16[128,4096]{1,0:T(8,128)(2,1)S(1)}) custom-call(bf16[16,64,7168]{2,1,0:T(8,128)(2,1)} %get-tuple-element.13.g_ref, bf16[2,128,4096]{2,1,0:T(8,128)(2,1)S(1)} %get-tuple-element.14.shares_ref), custom_call_target="tpu_custom_call" | custom-call | tf_op jit(solution)/shard_map/scatter_grads/pallas_call | solution.py:271
  177.5 1.0 copy.9
  178.5 1.2 copy.10
Async XLA Ops:
  0.6 1.2 copy-start
  1.9 1.2 copy-start.2
  3.0 77.1 %copy-start.1 = (bf16[128,4096]{1,0:T(8,128)(2,1)S(1)}, bf16[128,4096]{1,0:T(8,128)(2,1)}, u32[]{:S(2)}) copy-start(bf16[128,4096]{1,0:T(8,128)(2,1)} %refs_0_.1) | copy-start | bytes 3145732
  3.0 77.1 %copy-start.4 = (s32[4,28]{1,0:T(4,128)S(1)}, s32[4,28]{1,0:T(4,128)}, u32[]{:S(2)}) copy-start(s32[4,28]{1,0:T(4,128)} %table_ref.1) | copy-start | bytes 1348
  80.1 1.5 copy-start.3
